TPU v7x, 256 devices: a whole 4x4x8 slice. The times are simulated.
256 devices in a mesh: dom: 32 (over x, y, core), dest: 8 (over z).
Axes of the slice: x: 4, y: 4, z: 8, core: 2. Of those that a mesh axis runs over, the one named last changes fastest.
Arguments:
- cost: float32 [32768], P('dom'), may hold values from 0.2 to 1.5
- turn_weight: float32 [512, 64, 512], P('dom'), may hold values from 0.0005859375 to 0.01171875
- exit_value: float32 [384, 32768], P('dest', 'dom'), may hold values from 0.05 to 1
- demand: float32 [384, 32768], P('dest', 'dom'), may hold values from 0.02 to 1
- dest_weight: float32 [384], P('dest'), may hold values from 0.3 to 3
- slot_count: int32 [512], P('dom'), may hold values from 1 to 8
- col_ref: int32 [512, 8], P('dom'), may hold values from 0 to 79, as said below
- send_blocks: int32 [32, 32, 2], replicated, may hold values from 0 to 15
Outputs:
- flows: float32 [32768], P(('dom', 'dest'))
- cost_grad: float32 [32768], P(('dom', 'dest'))
Inputs may be any that keep to these rules, and one draw needn't show every extreme that they name: `col_ref`: A value below 16 names a block of the row block's own partition; a value 16 + p * 2 + c names block send_blocks[p, o, c] of partition p, o being the row block's partition.
All inputs are finite; a program needn't handle non-finite values.
Results may differ from a plain program's by a relative error of at most 0.0001.
Values sent between devices are 32-bit elements; how exact they have to be, the bound alone decides.
A program may use at most 128 MiB of HBM per device.

v0:
```python
import functools

import jax
import jax.numpy as jnp
from jax import lax
from jax.experimental import pallas as pl
from jax.experimental.pallas import tpu as pltpu
from jax.sharding import PartitionSpec as P

MESH = pl.DeviceIdType.MESH
BLK = 64
PAIR = 2 * BLK
SLOTS = 8
BLOCKS = 16
PARTS = 32
GROUPS = 8
DESTS = 48
CHUNKS = 2
ROWS = DESTS // CHUNKS
LIVE = BLOCKS * SLOTS
GHOSTS = 2 * PARTS
STAGES = 4


def hops(offset):
    dx, dy, dc = offset
    return min(dx, 4 - dx) + min(dy, 4 - dy) + 0.5 * dc


OFFSETS = sorted(
    ((dx, dy, dc) for dx in range(4) for dy in range(4) for dc in range(2) if dx or dy or dc),
    key=lambda o: -hops(o),
)
Z_OFFSETS = (4, 3, 5, 2, 6, 1, 7)


def split(v):
    high = v.astype(jnp.bfloat16)
    low = (v - high.astype(jnp.float32)).astype(jnp.bfloat16)
    return jnp.concatenate([high, low], axis=0)


def turn(v):
    return pltpu.roll(v, BLK, 1)


def kernel(
    cost_ref, exit_ref, demand_hbm, turn_hbm, weight_ref, count_ref, col_ref, outb_ref,
    flow_out, grad_out,
    turn_raw, demand_ref, matrix, table, exit_dup, weighted, value_dup, demand_dup, scale, dest_w,
    terms, scan, back_scan, local, returned, sort_v, sort_s,
    send, recv, z_part, z_recv,
    load_sem, send_sem, recv_sem, z_send_sem, z_recv_sem,
):
    me = lax.axis_index("dom")
    group = lax.axis_index("dest")
    x, y, c = me // 8, (me // 2) % 4, me % 2

    def partner(offset):
        dx, dy, dc = offset
        return (((x + dx) % 4) * 4 + (y + dy) % 4) * 2 + (c + dc) % 2

    barrier = pltpu.get_barrier_semaphore()
    for offset in OFFSETS:
        pl.semaphore_signal(barrier, inc=1, device_id=(partner(offset), group), device_id_type=MESH)
    for dz in Z_OFFSETS:
        pl.semaphore_signal(barrier, inc=1, device_id=(me, (group + dz) % GROUPS), device_id_type=MESH)

    turn_copy = pltpu.make_async_copy(turn_hbm, turn_raw, load_sem.at[0])
    turn_copy.start()
    demand_copy = pltpu.make_async_copy(demand_hbm, demand_ref, load_sem.at[1])
    demand_copy.start()

    lane = lax.broadcasted_iota(jnp.int32, (ROWS, PAIR), 1)
    low_half = lane < BLK
    half_of = lane // BLK
    low_half16 = lax.broadcasted_iota(jnp.int32, (2 * ROWS, PAIR), 1) < BLK

    def message(stage, chunk, make):
        for offset in OFFSETS:
            to = partner(offset)
            send[stage, chunk, to] = make(to)
            pltpu.make_async_remote_copy(
                src_ref=send.at[stage, chunk, to],
                dst_ref=recv.at[stage, chunk, me],
                send_sem=send_sem.at[stage, chunk],
                recv_sem=recv_sem.at[stage, chunk],
                device_id=(to, group),
                device_id_type=MESH,
            ).start()
        recv[stage, chunk, me] = make(me)

    def wait_received(stage, chunk):
        here = recv.at[stage, chunk, pl.ds(0, PARTS - 1)]
        pltpu.make_async_copy(here, here, recv_sem.at[stage, chunk]).wait()

    def forward_message(stage, chunk):
        def make(to):
            first, second = outb_ref[2 * to], outb_ref[2 * to + 1]
            return jnp.where(low_half, weighted[first], weighted[second])

        message(stage, chunk, make)

    def scale_row(n):
        return scale[n % 2, pl.ds(n // 2, 1), :]

    factor = jnp.exp(-cost_ref[...])
    turned = turn(factor)
    low8 = lax.broadcasted_iota(jnp.int32, (8, PAIR), 1) < BLK
    scale[0] = jnp.where(low8, factor, turned)
    scale[1] = jnp.where(low8, turned, factor)

    def rows_of(chunk):
        return pl.ds(pl.multiple_of(chunk * ROWS, 8), ROWS)

    def start_first(chunk):
        for m in range(BLOCKS // 2):
            pair = exit_ref[rows_of(chunk), m * PAIR : (m + 1) * PAIR]
            other = turn(pair)
            for h in range(2):
                dup = jnp.where(low_half, pair, other) if h == 0 else jnp.where(low_half, other, pair)
                exit_dup[chunk, 2 * m + h] = dup
                moved = dup * scale_row(2 * m + h)
                weighted[2 * m + h] = moved
                table[chunk, 2 * m + h] = split(moved)

    start_first(0)
    pl.semaphore_wait(barrier, len(OFFSETS) + len(Z_OFFSETS))
    forward_message(0, 0)

    @pl.loop(1, CHUNKS)
    def _(chunk):
        start_first(chunk)
        forward_message(0, chunk)

    turn_copy.wait()

    @pl.loop(0, BLOCKS)
    def _(n):
        column = lax.broadcasted_iota(jnp.int32, (BLK, SLOTS * BLK), 1)
        live = jnp.where(column < count_ref[n] * BLK, turn_raw[n], 0.0)
        matrix[n] = split(live)

    demand_copy.wait()

    @pl.loop(0, CHUNKS)
    def _(chunk):
        for m in range(BLOCKS // 2):
            pair = demand_ref[rows_of(chunk), m * PAIR : (m + 1) * PAIR]
            other = turn(pair)
            demand_dup[chunk, 2 * m] = jnp.where(low_half, pair, other)
            demand_dup[chunk, 2 * m + 1] = jnp.where(low_half, other, pair)

    @pl.loop(0, DESTS)
    def _(d):
        dest_w[pl.ds(d, 1), :] = jnp.full((1, PAIR), weight_ref[d], jnp.float32)

    square_lane = lax.broadcasted_iota(jnp.int32, (128, 128), 1)
    square_row = lax.broadcasted_iota(jnp.int32, (128, 128), 0)
    lane_row = lax.broadcasted_iota(jnp.int32, (1, 128), 1)

    def order(keys, total, at):
        def put(k, row):
            return jnp.where(lane_row == k, keys[k], row)

        row = lax.fori_loop(0, total, put, jnp.full((1, 128), 1000, jnp.int32))
        along = jnp.broadcast_to(row, (128, 128))
        down = along.T
        before = (along < down) | ((along == down) & (square_lane < square_row))
        rank = jnp.sum(jnp.where(before, 1, 0), axis=1, keepdims=True)
        hit = rank == square_lane
        entry = jnp.sum(jnp.where(hit, square_row, 0), axis=0, keepdims=True)
        key = jnp.sum(jnp.where(hit, down, 0), axis=0, keepdims=True)
        same = (key == pltpu.roll(key, 1, 1)) & (lane_row > 0)
        upto = jnp.sum(jnp.where(down <= square_lane, 1, 0), axis=0, keepdims=True)
        count = jnp.sum(jnp.where(down == square_lane, 1, 0), axis=0, keepdims=True)
        last = jnp.where(count > 0, upto - 1, total)
        sort_v[at : at + 1, :] = jnp.clip(entry, 0, total - 1)
        sort_v[at + 1 : at + 2, :] = jnp.where(same, 1, 0)
        sort_v[at + 2 : at + 3, :] = jnp.clip(last, 0, total)

    sort_v[...] = jnp.zeros_like(sort_v)
    order(col_ref, LIVE, 0)
    order(outb_ref, GHOSTS, 3)
    sort_copy = pltpu.make_async_copy(sort_v, sort_s, load_sem.at[2])
    sort_copy.start()
    sort_copy.wait()

    def run_sums(source, target, at, total):
        def step(k, running):
            entry = sort_s[at, k]
            found = jnp.where(half_of == entry % 2, source[entry // 2], 0.0)
            running = found + jnp.where(sort_s[at + 1, k] == 1, running, 0.0)
            target[k] = running
            return running

        lax.fori_loop(0, total, step, jnp.zeros((ROWS, PAIR), jnp.float32), unroll=8)

    scan[LIVE] = jnp.zeros((ROWS, PAIR), jnp.float32)
    back_scan[GHOSTS] = jnp.zeros((ROWS, PAIR), jnp.float32)

    def take_received(stage, chunk):
        @pl.loop(0, PARTS, unroll=4)
        def _(p):
            pair = recv[stage, chunk, p]
            other = turn(pair)
            table[chunk, BLOCKS + 2 * p] = split(jnp.where(low_half, pair, other))
            table[chunk, BLOCKS + 2 * p + 1] = split(jnp.where(low_half, other, pair))

    def product(chunk, n):
        picked = jnp.concatenate(
            [
                jnp.where(
                    low_half16,
                    table[chunk, col_ref[n * SLOTS + 2 * k]],
                    table[chunk, col_ref[n * SLOTS + 2 * k + 1]],
                )
                for k in range(SLOTS // 2)
            ],
            axis=1,
        )
        parts = lax.dot_general(
            picked, matrix[n], (((1,), (1,)), ((), ())), preferred_element_type=jnp.float32
        )
        both = parts[:ROWS] + parts[ROWS:]
        return both + turn(both)

    def adjoint_message(stage, chunk):
        run_sums(terms, scan, 0, LIVE)

        def make(to):
            first = scan[sort_s[2, BLOCKS + 2 * to]]
            second = scan[sort_s[2, BLOCKS + 2 * to + 1]]
            return jnp.where(low_half, first, second) + turn(jnp.where(low_half, second, first))

        message(stage, chunk, make)
        for b in range(BLOCKS):
            own = scan[sort_s[2, b]]
            local[chunk, b] = own + turn(own)

    def adjoint_product(n, ratio):
        parts = jnp.dot(split(ratio), matrix[n], preferred_element_type=jnp.float32)
        both = parts[:ROWS] + parts[ROWS:]
        for k in range(SLOTS // 2):
            terms[n * (SLOTS // 2) + k] = both[:, k * PAIR : (k + 1) * PAIR]

    @pl.loop(0, CHUNKS)
    def _(chunk):
        wait_received(0, chunk)
        take_received(0, chunk)
        for n in range(BLOCKS):
            value = product(chunk, n) + exit_dup[chunk, n]
            weighted[n] = value * scale_row(n)
        for n in range(BLOCKS):
            table[chunk, n] = split(weighted[n])
        forward_message(1, chunk)

    @pl.loop(0, CHUNKS)
    def _(chunk):
        wait_received(1, chunk)
        take_received(1, chunk)
        for n in range(BLOCKS):
            value = product(chunk, n) + exit_dup[chunk, n]
            value_dup[chunk, n] = value
            adjoint_product(n, demand_dup[chunk, n] / value)
        adjoint_message(2, chunk)

    def gather_back(stage, chunk):
        wait_received(stage, chunk)
        for p in range(PARTS):
            returned[p] = recv[stage, chunk, p]
        run_sums(returned, back_scan, 3, GHOSTS)

    def back_of(chunk, n):
        came = back_scan[sort_s[5, n]]
        return (local[chunk, n] + came + turn(came)) * scale_row(n)

    @pl.loop(0, CHUNKS)
    def _(chunk):
        gather_back(2, chunk)
        for n in range(BLOCKS):
            value = value_dup[chunk, n]
            load = value * back_of(chunk, n) + demand_dup[chunk, n]
            adjoint_product(n, load / value)
        adjoint_message(3, chunk)

    z_part[...] = jnp.zeros_like(z_part)
    low1 = lane_row < BLK

    @pl.loop(0, CHUNKS)
    def _(chunk):
        gather_back(3, chunk)
        weight = dest_w[rows_of(chunk), :]
        for g in range(GROUPS):
            flow, grad = [], []
            for h in range(2):
                n = 2 * g + h
                moved = value_dup[chunk, n] * back_of(chunk, n)
                flow.append(jnp.sum(moved + demand_dup[chunk, n], axis=0, keepdims=True))
                grad.append(jnp.sum(weight * moved, axis=0, keepdims=True))
            z_part[g, 0:1, :] += jnp.where(low1, flow[0], flow[1])
            z_part[g, 1:2, :] += jnp.where(low1, grad[0], grad[1])

    for dz in Z_OFFSETS:
        to = (group + dz) % GROUPS
        pltpu.make_async_remote_copy(
            src_ref=z_part.at[to],
            dst_ref=z_recv.at[group],
            send_sem=z_send_sem,
            recv_sem=z_recv_sem,
            device_id=(me, to),
            device_id_type=MESH,
        ).start()
    z_recv[group] = z_part[group]
    arrived = z_recv.at[pl.ds(0, GROUPS - 1)]
    pltpu.make_async_copy(arrived, arrived, z_recv_sem).wait()
    total = z_recv[0]
    for g in range(1, GROUPS):
        total = total + z_recv[g]
    total = total / (DESTS * GROUPS)
    flow_out[...] = total[0:1, :]
    grad_out[...] = -total[1:2, :]

    left = z_part.at[pl.ds(0, GROUPS - 1)]
    pltpu.make_async_copy(left, left, z_send_sem).wait()

    @pl.loop(0, STAGES)
    def _(stage):
        @pl.loop(0, CHUNKS)
        def _(chunk):
            gone = send.at[stage, chunk, pl.ds(0, PARTS - 1)]
            pltpu.make_async_copy(gone, gone, send_sem.at[stage, chunk]).wait()


def local_part(cost, turn_weight, exit_value, demand, dest_weight, slot_count, col_ref, send_blocks):
    me = lax.axis_index("dom")
    outbound = lax.dynamic_index_in_dim(send_blocks.reshape(PARTS, GHOSTS), me, 0, keepdims=False)
    vmem = pl.BlockSpec(memory_space=pltpu.VMEM)
    smem = pl.BlockSpec(memory_space=pltpu.SMEM)
    anywhere = pl.BlockSpec(memory_space=pl.ANY)
    f32, bf16 = jnp.float32, jnp.bfloat16
    flows, grad = pl.pallas_call(
        kernel,
        out_shape=(jax.ShapeDtypeStruct((1, PAIR), f32), jax.ShapeDtypeStruct((1, PAIR), f32)),
        in_specs=[vmem, vmem, anywhere, anywhere, smem, smem, smem, smem],
        out_specs=(vmem, vmem),
        scratch_shapes=[
            pltpu.VMEM((BLOCKS, BLK, SLOTS * BLK), f32),
            pltpu.VMEM((DESTS, BLOCKS * BLK), f32),
            pltpu.VMEM((BLOCKS, 2 * BLK, SLOTS * BLK), bf16),
            pltpu.VMEM((CHUNKS, BLOCKS + GHOSTS, 2 * ROWS, PAIR), bf16),
            pltpu.VMEM((CHUNKS, BLOCKS, ROWS, PAIR), f32),
            pltpu.VMEM((BLOCKS, ROWS, PAIR), f32),
            pltpu.VMEM((CHUNKS, BLOCKS, ROWS, PAIR), f32),
            pltpu.VMEM((CHUNKS, BLOCKS, ROWS, PAIR), f32),
            pltpu.VMEM((2, 8, PAIR), f32),
            pltpu.VMEM((DESTS, PAIR), f32),
            pltpu.VMEM((LIVE // 2, ROWS, PAIR), f32),
            pltpu.VMEM((LIVE + 1, ROWS, PAIR), f32),
            pltpu.VMEM((GHOSTS + 1, ROWS, PAIR), f32),
            pltpu.VMEM((CHUNKS, BLOCKS, ROWS, PAIR), f32),
            pltpu.VMEM((PARTS, ROWS, PAIR), f32),
            pltpu.VMEM((8, 128), jnp.int32),
            pltpu.SMEM((8, 128), jnp.int32),
            pltpu.VMEM((STAGES, CHUNKS, PARTS, ROWS, PAIR), f32),
            pltpu.VMEM((STAGES, CHUNKS, PARTS, ROWS, PAIR), f32),
            pltpu.VMEM((GROUPS, 8, PAIR), f32),
            pltpu.VMEM((GROUPS, 8, PAIR), f32),
            pltpu.SemaphoreType.DMA((3,)),
            pltpu.SemaphoreType.DMA((STAGES, CHUNKS)),
            pltpu.SemaphoreType.DMA((STAGES, CHUNKS)),
            pltpu.SemaphoreType.DMA,
            pltpu.SemaphoreType.DMA,
        ],
        compiler_params=pltpu.CompilerParams(
            collective_id=0, has_side_effects=True, vmem_limit_bytes=48 * 2**20
        ),
        name="route_choice",
    )(
        cost.reshape(8, PAIR), exit_value, demand, turn_weight, dest_weight, slot_count,
        col_ref.reshape(LIVE), outbound,
    )
    return flows.reshape(PAIR), grad.reshape(PAIR)


def solution(mesh):
    placed = (
        P("dom"),
        P("dom", None, None),
        P("dest", "dom"),
        P("dest", "dom"),
        P("dest"),
        P("dom"),
        P("dom", None),
        P(),
    )
    return jax.shard_map(
        local_part,
        mesh=mesh,
        in_specs=placed,
        out_specs=(P(("dom", "dest")), P(("dom", "dest"))),
        check_vma=False,
    )
```

profile of v0, /device:TPU:1, one launch (start us, length us, event | category | flops | bytes accessed | tf_op | source)
XLA Modules:
  0.0 76.8 jit_solution(9861284162352378800)
XLA Ops:
  0.6 0.8 %copy.14 = s32[32,32,2]{0,2,1:T(2,128)S(1)} copy(s32[32,32,2]{1,2,0:T(2,128)} %param.15) | data formatting | bytes 16384 | tf_op args[7]
  1.5 0.2 dynamic-slice_reduce_fusion.outb_ref
  1.7 0.8 copy.13
  2.4 0.1 reshape.20.col_ref
  2.5 0.0 copy-start
  2.5 1.6 %copy-done = f32[16,64,512]{2,1,0:T(8,128)S(1)} copy-done((f32[16,64,512]{2,1,0:T(8,128)S(1)}, f32[16,64,512]{2,1,0:T(8,128)}, u32[]{:S(2)}) %copy-start) | copy-done | bytes 2097176
  4.1 0.0 copy-start.1
  4.1 0.9 %copy-done.1 = f32[48,1024]{1,0:T(8,128)S(1)} copy-done((f32[48,1024]{1,0:T(8,128)S(1)}, f32[48,1024]{1,0:T(8,128)}, u32[]{:S(2)}) %copy-start.1) | copy-done | bytes 196632
  5.0 0.0 copy-start.2
  5.0 0.9 %copy-done.2 = f32[48,1024]{1,0:T(8,128)S(1)} copy-done((f32[48,1024]{1,0:T(8,128)S(1)}, f32[48,1024]{1,0:T(8,128)}, u32[]{:S(2)}) %copy-start.2) | copy-done | bytes 196632
  6.0 0.0 copy-start.3
  6.0 0.7 copy-done.3
  6.6 0.0 copy-start.4
  6.6 0.7 copy-done.4
  7.3 0.0 copy-start.5
  7.3 0.7 copy-done.5
  8.0 67.8 %route_choice.1 = (f32[1,128]{1,0:T(1,128)S(1)}, f32[1,128]{1,0:T(1,128)S(1)}) custom-call(f32[8,128]{1,0:T(8,128)S(1)} %bitcast.4, f32[48,1024]{1,0:T(8,128)S(1)} %copy-done.1, f32[48,1024]{1,0:T(8,128)S(1)} %copy-done.2, f32[16,64,512]{2,1,0:T(8,128)S(1)} %copy-done, f32[48]{0:T(128)S(1)} %copy-done.4, s32[16]{0:T(128)S(1)} %copy-done.5, ...), custom_call_target="tpu_custom_call" | custom-call | tf_op jit(solution)/shard_map/route_choice/pallas_call | solution.py:342
  75.8 0.5 copy.17
  76.3 0.5 copy.18
Async XLA Ops:
  2.5 1.6 %copy-start = (f32[16,64,512]{2,1,0:T(8,128)S(1)}, f32[16,64,512]{2,1,0:T(8,128)}, u32[]{:S(2)}) copy-start(f32[16,64,512]{2,1,0:T(8,128)} %turn_hbm.1) | copy-start | bytes 6291460
  4.1 0.9 %copy-start.1 = (f32[48,1024]{1,0:T(8,128)S(1)}, f32[48,1024]{1,0:T(8,128)}, u32[]{:S(2)}) copy-start(f32[48,1024]{1,0:T(8,128)} %exit_ref.1) | copy-start | bytes 589828
  5.0 0.9 %copy-start.2 = (f32[48,1024]{1,0:T(8,128)S(1)}, f32[48,1024]{1,0:T(8,128)}, u32[]{:S(2)}) copy-start(f32[48,1024]{1,0:T(8,128)} %demand_hbm.1) | copy-start | bytes 589828
  6.0 0.7 copy-start.3
  6.6 0.7 copy-start.4
  7.3 0.7 copy-start.5
where the time goes:
time: 77.1 us; the launch traced here: 76.8 us
  Pallas kernels  67.8 us (88%)
  local copies, waits for them, and re-layouts  8.33 us (11%)
    pallas_call x1, Pallas kernels, local_part(): pl.pallas_call(kernel, out_shape=(jax.ShapeDtypeStruct((1, PAIR), f32), j...  67.8 us
    unnamed x16, local copies, waits for them, and re-layouts  8.07 us

commit v1 on v0

v1 whole, which is shorter than its diff:
```python
import functools

import jax
import jax.numpy as jnp
from jax import lax
from jax.experimental import pallas as pl
from jax.experimental.pallas import tpu as pltpu
from jax.sharding import PartitionSpec as P

MESH = pl.DeviceIdType.MESH
BLK = 64
PAIR = 2 * BLK
SLOTS = 8
BLOCKS = 16
PARTS = 32
GROUPS = 8
DESTS = 48
CHUNKS = 3
ROWS = DESTS // CHUNKS
LIVE = BLOCKS * SLOTS
GHOSTS = 2 * PARTS
STAGES = 4


def hops(offset):
    dx, dy, dc = offset
    return min(dx, 4 - dx) + min(dy, 4 - dy) + 0.5 * dc


OFFSETS = sorted(
    ((dx, dy, dc) for dx in range(4) for dy in range(4) for dc in range(2) if dx or dy or dc),
    key=lambda o: -hops(o),
)
Z_OFFSETS = (4, 3, 5, 2, 6, 1, 7)


def split(v):
    high = v.astype(jnp.bfloat16)
    low = (v - high.astype(jnp.float32)).astype(jnp.bfloat16)
    return jnp.concatenate([high, low], axis=0)


def turn(v):
    return pltpu.roll(v, BLK, 1)


def kernel(
    cost_hbm, exit_hbm, demand_hbm, turn_hbm, weight_hbm, count_hbm, col_hbm, send_blocks_hbm,
    flow_out, grad_out,
    turn_raw, exit_ref, demand_ref, cost_ref, weight_ref, count_ref, col_ref, outb_ref,
    matrix, across, table, picked, parts, ratios, exit_dup, weighted, value_dup, demand_dup, scale, dest_w,
    terms, scan, back_scan, keep, back_keep, local, returned, sort_v, sort_s,
    send, recv, z_part, z_recv,
    load_sem, send_sem, recv_sem, z_send_sem, z_recv_sem,
):
    me = lax.axis_index("dom")
    group = lax.axis_index("dest")
    x, y, c = me // 8, (me // 2) % 4, me % 2

    def partner(offset):
        dx, dy, dc = offset
        return (((x + dx) % 4) * 4 + (y + dy) % 4) * 2 + (c + dc) % 2

    loads = [
        pltpu.make_async_copy(source, target, load_sem.at[i])
        for i, (source, target) in enumerate(
            (
                (cost_hbm, cost_ref),
                (exit_hbm, exit_ref),
                (send_blocks_hbm.at[me], outb_ref),
                (turn_hbm, turn_raw),
                (demand_hbm, demand_ref),
                (col_hbm, col_ref),
                (count_hbm, count_ref),
                (weight_hbm, weight_ref),
            )
        )
    ]
    for load in loads:
        load.start()

    barrier = pltpu.get_barrier_semaphore()
    for offset in OFFSETS:
        pl.semaphore_signal(barrier, inc=1, device_id=(partner(offset), group), device_id_type=MESH)
    for dz in Z_OFFSETS:
        pl.semaphore_signal(barrier, inc=1, device_id=(me, (group + dz) % GROUPS), device_id_type=MESH)

    lane = lax.broadcasted_iota(jnp.int32, (ROWS, PAIR), 1)
    low_half = lane < BLK
    low_half16 = lax.broadcasted_iota(jnp.int32, (2 * ROWS, PAIR), 1) < BLK
    lane_row = lax.broadcasted_iota(jnp.int32, (1, PAIR), 1)
    low1 = lane_row < BLK

    def message(stage, chunk, make):
        for offset in OFFSETS:
            to = partner(offset)
            send[stage, chunk, to] = make(to)
            pltpu.make_async_remote_copy(
                src_ref=send.at[stage, chunk, to],
                dst_ref=recv.at[stage, chunk, me],
                send_sem=send_sem.at[stage, chunk],
                recv_sem=recv_sem.at[stage, chunk],
                device_id=(to, group),
                device_id_type=MESH,
            ).start()
        recv[stage, chunk, me] = make(me)

    def wait_received(stage, chunk):
        here = recv.at[stage, chunk, pl.ds(0, PARTS - 1)]
        pltpu.make_async_copy(here, here, recv_sem.at[stage, chunk]).wait()

    def forward_message(stage, chunk):
        def make(to):
            return jnp.where(low_half, weighted[outb_ref[0, to]], weighted[outb_ref[1, to]])

        message(stage, chunk, make)

    def scale_row(n):
        return scale[n : n + 1, :]

    def rows_of(chunk):
        return pl.ds(pl.multiple_of(chunk * ROWS, 8), ROWS)

    def start_first(chunk):
        for m in range(BLOCKS // 2):
            pair = exit_ref[rows_of(chunk), m * PAIR : (m + 1) * PAIR]
            other = turn(pair)
            for h in range(2):
                n = 2 * m + h
                dup = jnp.where(low_half, pair, other) if h == 0 else jnp.where(low_half, other, pair)
                exit_dup[chunk, n] = dup
                moved = dup * scale_row(n)
                weighted[n] = moved
                table[chunk, n] = split(moved)

    loads[0].wait()
    for m in range(BLOCKS // 2):
        factor = jnp.exp(-cost_ref[pl.ds(m * PAIR, PAIR)].reshape(1, PAIR))
        turned = turn(factor)
        scale[2 * m : 2 * m + 1, :] = jnp.where(low1, factor, turned)
        scale[2 * m + 1 : 2 * m + 2, :] = jnp.where(low1, turned, factor)
    loads[1].wait()
    loads[2].wait()
    start_first(0)
    pl.semaphore_wait(barrier, len(OFFSETS) + len(Z_OFFSETS))
    forward_message(0, 0)

    @pl.loop(1, CHUNKS)
    def _(chunk):
        start_first(chunk)
        forward_message(0, chunk)

    for load in loads[3:]:
        load.wait()

    square_lane = lax.broadcasted_iota(jnp.int32, (128, 128), 1)
    square_row = lax.broadcasted_iota(jnp.int32, (128, 128), 0)

    def order(keys, half, at, keep_ref):
        odd = lane_row >= half
        row = jnp.where(lane_row < 2 * half, keys + jnp.where(odd, 256, 0), 4096)
        along = jnp.broadcast_to(row, (128, 128))
        down = along.T
        before = (along < down) | ((along == down) & (square_lane < square_row))
        rank = jnp.sum(jnp.where(before, 1, 0), axis=1, keepdims=True)
        hit = rank == square_lane
        entry = jnp.sum(jnp.where(hit, square_row, 0), axis=0, keepdims=True)
        key = jnp.sum(jnp.where(hit, down, 0), axis=0, keepdims=True)
        same = (key == pltpu.roll(key, 1, 1)) & (lane_row > 0)
        kept = jnp.broadcast_to(jnp.where(same, 1.0, 0.0), (128, 128)).T
        keep_ref[...] = jnp.where(low1, kept[:half], kept[half : 2 * half])
        sort_v[at : at + 1, :] = jnp.clip(entry - jnp.where(odd, half, 0), 0, half - 1)
        for h in range(2):
            target = square_lane + 256 * h
            upto = jnp.sum(jnp.where(down <= target, 1, 0), axis=0, keepdims=True)
            count = jnp.sum(jnp.where(down == target, 1, 0), axis=0, keepdims=True)
            last = jnp.where(count > 0, upto - 1 - half * h, half)
            sort_v[at + 1 + h : at + 2 + h, :] = jnp.clip(last, 0, half)

    def col_key(n, row):
        for s in range(SLOTS):
            at = (s % 2) * (LIVE // 2) + n * (SLOTS // 2) + s // 2
            row = jnp.where(lane_row == at, col_ref[s, n], row)
        return row

    def out_key(q, row):
        for h in range(2):
            row = jnp.where(lane_row == h * PARTS + q, outb_ref[h, q], row)
        return row

    col_row = lax.fori_loop(0, BLOCKS, col_key, jnp.zeros((1, 128), jnp.int32))
    out_row = lax.fori_loop(0, PARTS, out_key, jnp.zeros((1, 128), jnp.int32))
    sort_v[...] = jnp.zeros_like(sort_v)
    order(col_row, LIVE // 2, 1, keep)
    order(out_row, PARTS, 4, back_keep)
    swapped = (col_row >= BLOCKS) & (lane_row >= LIVE // 2)
    sort_v[0:1, :] = jnp.where(swapped, col_row + 1 - 2 * (col_row % 2), col_row)
    sort_copy = pltpu.make_async_copy(sort_v, sort_s, load_sem.at[0])
    sort_copy.start()

    @pl.loop(0, BLOCKS)
    def _(n):
        column = lax.broadcasted_iota(jnp.int32, (BLK, SLOTS * BLK), 1)
        live = jnp.where(column < count_ref[n] * BLK, turn_raw[n], 0.0)
        both = split(live)
        matrix[n] = both
        across[n] = both.T

    @pl.loop(0, CHUNKS)
    def _(chunk):
        for m in range(BLOCKS // 2):
            pair = demand_ref[rows_of(chunk), m * PAIR : (m + 1) * PAIR]
            other = turn(pair)
            demand_dup[chunk, 2 * m] = jnp.where(low_half, pair, other)
            demand_dup[chunk, 2 * m + 1] = jnp.where(low_half, other, pair)

    @pl.loop(0, DESTS)
    def _(d):
        dest_w[pl.ds(d, 1), :] = jnp.full((1, PAIR), weight_ref[d], jnp.float32)

    sort_copy.wait()
    scan[LIVE // 2] = jnp.zeros((ROWS, PAIR), jnp.float32)
    back_scan[PARTS] = jnp.zeros((ROWS, PAIR), jnp.float32)
    z_part[...] = jnp.zeros_like(z_part)

    def run_sums(source, keep_ref, target, at, half):
        def step(k, running):
            even, odd = source[sort_s[at, k]], source[sort_s[at, half + k]]
            running = jnp.where(low_half, even, odd) + keep_ref[pl.ds(k, 1), :] * running
            target[k] = running
            return running

        lax.fori_loop(0, half, step, jnp.zeros((ROWS, PAIR), jnp.float32), unroll=16)

    def sums_at(source, at, first, second):
        return jnp.where(low_half, source[sort_s[at, first]], source[sort_s[at + 1, second]])

    def take_received(stage, chunk):
        @pl.loop(0, PARTS, unroll=8)
        def _(p):
            pair = recv[stage, chunk, p]
            table[chunk, BLOCKS + 2 * p] = split(pair)
            table[chunk, BLOCKS + 2 * p + 1] = split(turn(pair))

    def products(stage, chunk):
        wait_received(stage, chunk)
        take_received(stage, chunk)
        half = SLOTS // 2
        for n in range(BLOCKS):
            for k in range(half):
                even = table[chunk, sort_s[0, n * half + k]]
                odd = table[chunk, sort_s[0, LIVE // 2 + n * half + k]]
                picked[n, :, k * PAIR : (k + 1) * PAIR] = jnp.where(low_half16, even, odd)
        for n in range(BLOCKS):
            parts[n] = jnp.dot(picked[n], across[n], preferred_element_type=jnp.float32)

    def value_of(chunk, n):
        both = parts[n, :ROWS] + parts[n, ROWS:]
        return both + turn(both) + exit_dup[chunk, n]

    def adjoint_message(stage, chunk):
        half = SLOTS // 2
        for n in range(BLOCKS):
            out = jnp.dot(ratios[n], matrix[n], preferred_element_type=jnp.float32)
            both = out[:ROWS] + out[ROWS:]
            for k in range(half):
                terms[n * half + k] = both[:, k * PAIR : (k + 1) * PAIR]
        run_sums(terms, keep, scan, 1, LIVE // 2)

        def make(to):
            first = BLOCKS + 2 * to
            return sums_at(scan, 2, first, first + 1) + turn(sums_at(scan, 2, first + 1, first))

        message(stage, chunk, make)
        for b in range(BLOCKS):
            own = sums_at(scan, 2, b, b)
            local[chunk, b] = own + turn(own)

    @pl.loop(0, CHUNKS)
    def _(chunk):
        products(0, chunk)
        for n in range(BLOCKS):
            moved = value_of(chunk, n) * scale_row(n)
            weighted[n] = moved
            table[chunk, n] = split(moved)
        forward_message(1, chunk)

    @pl.loop(0, CHUNKS)
    def _(chunk):
        products(1, chunk)
        for n in range(BLOCKS):
            value = value_of(chunk, n)
            value_dup[chunk, n] = value
            ratios[n] = split(demand_dup[chunk, n] / value)
        adjoint_message(2, chunk)

    def gather_back(stage, chunk):
        wait_received(stage, chunk)
        for p in range(PARTS):
            returned[p] = recv[stage, chunk, p]
        run_sums(returned, back_keep, back_scan, 4, PARTS)

    def back_of(chunk, n):
        came = sums_at(back_scan, 5, n, n)
        return (local[chunk, n] + came + turn(came)) * scale_row(n)

    @pl.loop(0, CHUNKS)
    def _(chunk):
        gather_back(2, chunk)
        for n in range(BLOCKS):
            value = value_dup[chunk, n]
            load = value * back_of(chunk, n) + demand_dup[chunk, n]
            ratios[n] = split(load / value)
        adjoint_message(3, chunk)

    @pl.loop(0, CHUNKS)
    def _(chunk):
        gather_back(3, chunk)
        weight = dest_w[rows_of(chunk), :]
        for g in range(GROUPS):
            flow, grad = [], []
            for h in range(2):
                n = 2 * g + h
                moved = value_dup[chunk, n] * back_of(chunk, n)
                flow.append(jnp.sum(moved + demand_dup[chunk, n], axis=0, keepdims=True))
                grad.append(jnp.sum(weight * moved, axis=0, keepdims=True))
            z_part[g, 0:1, :] += jnp.where(low1, flow[0], flow[1])
            z_part[g, 1:2, :] += jnp.where(low1, grad[0], grad[1])

    for dz in Z_OFFSETS:
        to = (group + dz) % GROUPS
        pltpu.make_async_remote_copy(
            src_ref=z_part.at[to],
            dst_ref=z_recv.at[group],
            send_sem=z_send_sem,
            recv_sem=z_recv_sem,
            device_id=(me, to),
            device_id_type=MESH,
        ).start()
    z_recv[group] = z_part[group]
    arrived = z_recv.at[pl.ds(0, GROUPS - 1)]
    pltpu.make_async_copy(arrived, arrived, z_recv_sem).wait()
    total = z_recv[0]
    for g in range(1, GROUPS):
        total = total + z_recv[g]
    total = total / (DESTS * GROUPS)
    flow_out[...] = total[0:1, :]
    grad_out[...] = -total[1:2, :]

    left = z_part.at[pl.ds(0, GROUPS - 1)]
    pltpu.make_async_copy(left, left, z_send_sem).wait()

    @pl.loop(0, STAGES)
    def _(stage):
        @pl.loop(0, CHUNKS)
        def _(chunk):
            gone = send.at[stage, chunk, pl.ds(0, PARTS - 1)]
            pltpu.make_async_copy(gone, gone, send_sem.at[stage, chunk]).wait()


def local_part(cost, turn_weight, exit_value, demand, dest_weight, slot_count, col_ref, send_blocks):
    vmem = pl.BlockSpec(memory_space=pltpu.VMEM)
    anywhere = pl.BlockSpec(memory_space=pl.ANY)
    f32, bf16 = jnp.float32, jnp.bfloat16
    flows, grad = pl.pallas_call(
        kernel,
        out_shape=(jax.ShapeDtypeStruct((1, PAIR), f32), jax.ShapeDtypeStruct((1, PAIR), f32)),
        in_specs=[anywhere] * 8,
        out_specs=(vmem, vmem),
        scratch_shapes=[
            pltpu.VMEM((BLOCKS, BLK, SLOTS * BLK), f32),
            pltpu.VMEM((DESTS, BLOCKS * BLK), f32),
            pltpu.VMEM((DESTS, BLOCKS * BLK), f32),
            pltpu.VMEM((BLOCKS * BLK,), f32),
            pltpu.SMEM((DESTS,), f32),
            pltpu.SMEM((BLOCKS,), jnp.int32),
            pltpu.SMEM((SLOTS, BLOCKS), jnp.int32),
            pltpu.SMEM((2, PARTS), jnp.int32),
            pltpu.VMEM((BLOCKS, 2 * BLK, SLOTS * BLK), bf16),
            pltpu.VMEM((BLOCKS, SLOTS * BLK, 2 * BLK), bf16),
            pltpu.VMEM((CHUNKS, BLOCKS + GHOSTS, 2 * ROWS, PAIR), bf16),
            pltpu.VMEM((BLOCKS, 2 * ROWS, SLOTS * BLK), bf16),
            pltpu.VMEM((BLOCKS, 2 * ROWS, PAIR), f32),
            pltpu.VMEM((BLOCKS, 2 * ROWS, PAIR), bf16),
            pltpu.VMEM((CHUNKS, BLOCKS, ROWS, PAIR), f32),
            pltpu.VMEM((BLOCKS, ROWS, PAIR), f32),
            pltpu.VMEM((CHUNKS, BLOCKS, ROWS, PAIR), f32),
            pltpu.VMEM((CHUNKS, BLOCKS, ROWS, PAIR), f32),
            pltpu.VMEM((BLOCKS, PAIR), f32),
            pltpu.VMEM((DESTS, PAIR), f32),
            pltpu.VMEM((LIVE // 2, ROWS, PAIR), f32),
            pltpu.VMEM((LIVE // 2 + 1, ROWS, PAIR), f32),
            pltpu.VMEM((PARTS + 1, ROWS, PAIR), f32),
            pltpu.VMEM((LIVE // 2, PAIR), f32),
            pltpu.VMEM((PARTS, PAIR), f32),
            pltpu.VMEM((CHUNKS, BLOCKS, ROWS, PAIR), f32),
            pltpu.VMEM((PARTS, ROWS, PAIR), f32),
            pltpu.VMEM((8, 128), jnp.int32),
            pltpu.SMEM((8, 128), jnp.int32),
            pltpu.VMEM((STAGES, CHUNKS, PARTS, ROWS, PAIR), f32),
            pltpu.VMEM((STAGES, CHUNKS, PARTS, ROWS, PAIR), f32),
            pltpu.VMEM((GROUPS, 8, PAIR), f32),
            pltpu.VMEM((GROUPS, 8, PAIR), f32),
            pltpu.SemaphoreType.DMA((8,)),
            pltpu.SemaphoreType.DMA((STAGES, CHUNKS)),
            pltpu.SemaphoreType.DMA((STAGES, CHUNKS)),
            pltpu.SemaphoreType.DMA,
            pltpu.SemaphoreType.DMA,
        ],
        compiler_params=pltpu.CompilerParams(
            collective_id=0, has_side_effects=True, vmem_limit_bytes=60 * 2**20
        ),
        name="route_choice",
    )(
        cost, exit_value, demand, turn_weight, dest_weight, slot_count, col_ref.T,
        send_blocks.transpose(0, 2, 1),
    )
    return flows.reshape(PAIR), grad.reshape(PAIR)


def solution(mesh):
    placed = (
        P("dom"),
        P("dom", None, None),
        P("dest", "dom"),
        P("dest", "dom"),
        P("dest"),
        P("dom"),
        P("dom", None),
        P(),
    )
    return jax.shard_map(
        local_part,
        mesh=mesh,
        in_specs=placed,
        out_specs=(P(("dom", "dest")), P(("dom", "dest"))),
        check_vma=False,
    )
```

time: 77.1 us -> 59.1 us (0.77)
  Pallas kernels: 67.8 us -> 56 us
  local copies, waits for them, and re-layouts: 8.33 us -> 2.25 us
    pallas_call x1, Pallas kernels: 67.8 us -> 56 us  [local_part(): pl.pallas_call(kernel, out_shape=(jax.ShapeDtypeStruct((1, PAIR), f32), j...]
    unnamed x16 -> x2, local copies, waits for them, and re-layouts: 8.07 us -> 2.25 us
where the time goes in v1:
time: 59.1 us; the launch traced here: 58.9 us
  Pallas kernels  56 us (95%)
  local copies, waits for them, and re-layouts  2.25 us (4%)
  between operations  0.64 us (1%)
    pallas_call x1, Pallas kernels, local_part(): pl.pallas_call(kernel, out_shape=(jax.ShapeDtypeStruct((1, PAIR), f32), j...  56 us
    unnamed x2, local copies, waits for them, and re-layouts  2.25 us

profile of v1, /device:TPU:1, one launch (start us, length us, event | category | flops | bytes accessed | tf_op | source)
XLA Modules:
  0.0 58.9 jit_solution(8376131711084908717)
XLA Ops:
  0.6 56.0 %route_choice.1 = (f32[1,128]{1,0:T(1,128)}, f32[1,128]{1,0:T(1,128)}) custom-call(f32[1024]{0:T(1024)} %cost_hbm.1, f32[48,1024]{1,0:T(8,128)} %exit_hbm.1, f32[48,1024]{1,0:T(8,128)} %demand_hbm.1, f32[16,64,512]{2,1,0:T(8,128)} %turn_hbm.1, f32[48]{0:T(128)} %weight_hbm.1, s32[16]{0:T(128)} %count_hbm.1, s32[8,16]{1,0:T(8,128)} %bitcast.5, ...), custom_call_target="tpu_custom_call" | custom-call | tf_op jit(solution)/shard_map/route_choice/pallas_call | solution.py:365
  56.7 1.1 %copy.12 = f32[128]{0:T(128)} copy(f32[128]{0:T(128)} %bitcast.7) | data formatting | bytes 1024
  57.8 1.1 %copy.13 = f32[128]{0:T(128)} copy(f32[128]{0:T(128)} %bitcast.6) | data formatting | bytes 1024

commit v2 on v1

--- a/solution.py
+++ b/solution.py
@@ -46,10 +46,10 @@
 
 def kernel(
     cost_hbm, exit_hbm, demand_hbm, turn_hbm, weight_hbm, count_hbm, col_hbm, send_blocks_hbm,
-    flow_out, grad_out,
+    out_ref,
     turn_raw, exit_ref, demand_ref, cost_ref, weight_ref, count_ref, col_ref, outb_ref,
     matrix, across, table, picked, parts, ratios, exit_dup, weighted, value_dup, demand_dup, scale, dest_w,
-    terms, scan, back_scan, keep, back_keep, local, returned, sort_v, sort_s,
+    terms, scan, back_scan, keep, back_keep, local, returned, sort_v, sort_s, out_at, sum_at,
     send, recv, z_part, z_recv,
     load_sem, send_sem, recv_sem, z_send_sem, z_recv_sem,
 ):
@@ -57,9 +57,13 @@
     group = lax.axis_index("dest")
     x, y, c = me // 8, (me // 2) % 4, me % 2
 
+    along_x = [8 * ((x + d) % 4) for d in range(4)]
+    along_y = [2 * ((y + d) % 4) for d in range(4)]
+    core = (c, 1 - c)
+
     def partner(offset):
         dx, dy, dc = offset
-        return (((x + dx) % 4) * 4 + (y + dy) % 4) * 2 + (c + dc) % 2
+        return along_x[dx] + along_y[dy] + core[dc]
 
     loads = [
         pltpu.make_async_copy(source, target, load_sem.at[i])
@@ -76,7 +80,7 @@
             )
         )
     ]
-    for load in loads:
+    for load in loads[:3]:
         load.start()
 
     barrier = pltpu.get_barrier_semaphore()
@@ -85,6 +89,9 @@
     for dz in Z_OFFSETS:
         pl.semaphore_signal(barrier, inc=1, device_id=(me, (group + dz) % GROUPS), device_id_type=MESH)
 
+    for load in loads[3:]:
+        load.start()
+
     lane = lax.broadcasted_iota(jnp.int32, (ROWS, PAIR), 1)
     low_half = lane < BLK
     low_half16 = lax.broadcasted_iota(jnp.int32, (2 * ROWS, PAIR), 1) < BLK
@@ -92,28 +99,32 @@
     low1 = lane_row < BLK
 
     def message(stage, chunk, make):
-        for offset in OFFSETS:
+        for i, offset in enumerate(OFFSETS):
             to = partner(offset)
-            send[stage, chunk, to] = make(to)
+            send[stage, chunk, i] = make(i)
             pltpu.make_async_remote_copy(
-                src_ref=send.at[stage, chunk, to],
+                src_ref=send.at[stage, chunk, i],
                 dst_ref=recv.at[stage, chunk, me],
                 send_sem=send_sem.at[stage, chunk],
                 recv_sem=recv_sem.at[stage, chunk],
                 device_id=(to, group),
                 device_id_type=MESH,
             ).start()
-        recv[stage, chunk, me] = make(me)
+        recv[stage, chunk, me] = make(PARTS - 1)
 
     def wait_received(stage, chunk):
         here = recv.at[stage, chunk, pl.ds(0, PARTS - 1)]
         pltpu.make_async_copy(here, here, recv_sem.at[stage, chunk]).wait()
 
     def forward_message(stage, chunk):
-        def make(to):
-            return jnp.where(low_half, weighted[outb_ref[0, to]], weighted[outb_ref[1, to]])
+        def make(i):
+            return jnp.where(low_half, weighted[out_at[2 * i]], weighted[out_at[2 * i + 1]])
 
         message(stage, chunk, make)
+
+    def own_table(chunk):
+        for n in range(BLOCKS):
+            table[chunk, n] = split(weighted[n])
 
     def scale_row(n):
         return scale[n : n + 1, :]
@@ -129,9 +140,7 @@
                 n = 2 * m + h
                 dup = jnp.where(low_half, pair, other) if h == 0 else jnp.where(low_half, other, pair)
                 exit_dup[chunk, n] = dup
-                moved = dup * scale_row(n)
-                weighted[n] = moved
-                table[chunk, n] = split(moved)
+                weighted[n] = dup * scale_row(n)
 
     loads[0].wait()
     for m in range(BLOCKS // 2):
@@ -139,16 +148,22 @@
         turned = turn(factor)
         scale[2 * m : 2 * m + 1, :] = jnp.where(low1, factor, turned)
         scale[2 * m + 1 : 2 * m + 2, :] = jnp.where(low1, turned, factor)
+    loads[2].wait()
+    for i, offset in enumerate((*OFFSETS, (0, 0, 0))):
+        to = partner(offset)
+        for h in range(2):
+            out_at[2 * i + h] = outb_ref[h, to]
     loads[1].wait()
-    loads[2].wait()
     start_first(0)
     pl.semaphore_wait(barrier, len(OFFSETS) + len(Z_OFFSETS))
     forward_message(0, 0)
+    own_table(0)
 
     @pl.loop(1, CHUNKS)
     def _(chunk):
         start_first(chunk)
         forward_message(0, chunk)
+        own_table(chunk)
 
     for load in loads[3:]:
         load.wait()
@@ -219,18 +234,21 @@
         dest_w[pl.ds(d, 1), :] = jnp.full((1, PAIR), weight_ref[d], jnp.float32)
 
     sort_copy.wait()
+    for i, offset in enumerate((*OFFSETS, (0, 0, 0))):
+        first = BLOCKS + 2 * partner(offset)
+        sum_at[4 * i] = sort_s[2, first]
+        sum_at[4 * i + 1] = sort_s[3, first + 1]
+        sum_at[4 * i + 2] = sort_s[2, first + 1]
+        sum_at[4 * i + 3] = sort_s[3, first]
     scan[LIVE // 2] = jnp.zeros((ROWS, PAIR), jnp.float32)
     back_scan[PARTS] = jnp.zeros((ROWS, PAIR), jnp.float32)
     z_part[...] = jnp.zeros_like(z_part)
 
     def run_sums(source, keep_ref, target, at, half):
-        def step(k, running):
-            even, odd = source[sort_s[at, k]], source[sort_s[at, half + k]]
-            running = jnp.where(low_half, even, odd) + keep_ref[pl.ds(k, 1), :] * running
+        for k in range(half):
+            found = jnp.where(low_half, source[sort_s[at, k]], source[sort_s[at, half + k]])
+            running = found if k == 0 else found + keep_ref[k : k + 1, :] * running
             target[k] = running
-            return running
-
-        lax.fori_loop(0, half, step, jnp.zeros((ROWS, PAIR), jnp.float32), unroll=16)
 
     def sums_at(source, at, first, second):
         return jnp.where(low_half, source[sort_s[at, first]], source[sort_s[at + 1, second]])
@@ -267,9 +285,9 @@
                 terms[n * half + k] = both[:, k * PAIR : (k + 1) * PAIR]
         run_sums(terms, keep, scan, 1, LIVE // 2)
 
-        def make(to):
-            first = BLOCKS + 2 * to
-            return sums_at(scan, 2, first, first + 1) + turn(sums_at(scan, 2, first + 1, first))
+        def make(i):
+            one, two, three, four = (scan[sum_at[4 * i + j]] for j in range(4))
+            return jnp.where(low_half, one, two) + turn(jnp.where(low_half, three, four))
 
         message(stage, chunk, make)
         for b in range(BLOCKS):
@@ -280,10 +298,9 @@
     def _(chunk):
         products(0, chunk)
         for n in range(BLOCKS):
-            moved = value_of(chunk, n) * scale_row(n)
-            weighted[n] = moved
-            table[chunk, n] = split(moved)
+            weighted[n] = value_of(chunk, n) * scale_row(n)
         forward_message(1, chunk)
+        own_table(chunk)
 
     @pl.loop(0, CHUNKS)
     def _(chunk):
@@ -343,9 +360,7 @@
     total = z_recv[0]
     for g in range(1, GROUPS):
         total = total + z_recv[g]
-    total = total / (DESTS * GROUPS)
-    flow_out[...] = total[0:1, :]
-    grad_out[...] = -total[1:2, :]
+    out_ref[...] = total / (DESTS * GROUPS)
 
     left = z_part.at[pl.ds(0, GROUPS - 1)]
     pltpu.make_async_copy(left, left, z_send_sem).wait()
@@ -362,11 +377,11 @@
     vmem = pl.BlockSpec(memory_space=pltpu.VMEM)
     anywhere = pl.BlockSpec(memory_space=pl.ANY)
     f32, bf16 = jnp.float32, jnp.bfloat16
-    flows, grad = pl.pallas_call(
+    both = pl.pallas_call(
         kernel,
-        out_shape=(jax.ShapeDtypeStruct((1, PAIR), f32), jax.ShapeDtypeStruct((1, PAIR), f32)),
+        out_shape=jax.ShapeDtypeStruct((8, PAIR), f32),
         in_specs=[anywhere] * 8,
-        out_specs=(vmem, vmem),
+        out_specs=vmem,
         scratch_shapes=[
             pltpu.VMEM((BLOCKS, BLK, SLOTS * BLK), f32),
             pltpu.VMEM((DESTS, BLOCKS * BLK), f32),
@@ -397,6 +412,8 @@
             pltpu.VMEM((PARTS, ROWS, PAIR), f32),
             pltpu.VMEM((8, 128), jnp.int32),
             pltpu.SMEM((8, 128), jnp.int32),
+            pltpu.SMEM((2 * PARTS,), jnp.int32),
+            pltpu.SMEM((4 * PARTS,), jnp.int32),
             pltpu.VMEM((STAGES, CHUNKS, PARTS, ROWS, PAIR), f32),
             pltpu.VMEM((STAGES, CHUNKS, PARTS, ROWS, PAIR), f32),
             pltpu.VMEM((GROUPS, 8, PAIR), f32),
@@ -415,7 +432,7 @@
         cost, exit_value, demand, turn_weight, dest_weight, slot_count, col_ref.T,
         send_blocks.transpose(0, 2, 1),
     )
-    return flows.reshape(PAIR), grad.reshape(PAIR)
+    return both[0], -both[1]
 
 
 def solution(mesh):

time: 59.1 us -> 56.7 us (0.959)
  local copies, waits for them, and re-layouts: 2.25 us -> 0 us
  Pallas kernels: 56 us -> 54.6 us
  other arithmetic: 0 us -> 1.26 us
    unnamed x2 -> x0, local copies, waits for them, and re-layouts: 2.25 us -> none
    pallas_call x1, Pallas kernels: 56 us -> 54.6 us  [local_part(): pl.pallas_call(kernel, out_shape=jax.ShapeDtypeStruct((8, PAIR), f32), in...]
    neg x0 -> x1, other arithmetic: none -> 1.26 us  [local_part(): return (both[0], -both[1])]
where the time goes in v2:
time: 56.7 us; the launch traced here: 56.5 us
  Pallas kernels  54.6 us (96%)
  other arithmetic  1.26 us (2%)
  between operations  0.64 us (1%)
    pallas_call x1, Pallas kernels, local_part(): pl.pallas_call(kernel, out_shape=jax.ShapeDtypeStruct((8, PAIR), f32), in...  54.6 us
    neg x1, other arithmetic, local_part(): return (both[0], -both[1])  1.26 us

profile of v2, /device:TPU:1, one launch (start us, length us, event | category | flops | bytes accessed | tf_op | source)
XLA Modules:
  0.0 56.5 jit_solution(9791912152932735124)
XLA Ops:
  0.6 54.6 %route_choice.1 = f32[8,128]{1,0:T(8,128)} custom-call(f32[1024]{0:T(1024)} %cost_hbm.1, f32[48,1024]{1,0:T(8,128)} %exit_hbm.1, f32[48,1024]{1,0:T(8,128)} %demand_hbm.1, f32[16,64,512]{2,1,0:T(8,128)} %turn_hbm.1, f32[48]{0:T(128)} %weight_hbm.1, s32[16]{0:T(128)} %count_hbm.1, s32[8,16]{1,0:T(8,128)} %bitcast.7, s32[32,2,32]{2,1,0:T(2,128)} %bitcast.6), custom_call_target="tpu_custom_call" | custom-call | tf_op jit(solution)/shard_map/route_choice/pallas_call | solution.py:380
  55.3 1.3 %negate_bitcast_fusion = (f32[128]{0:T(128)}, f32[128]{0:T(128)}) fusion(f32[8,128]{1,0:T(8,128)} %route_choice.1), kind=kLoop, calls=%fused_computation | loop fusion | flops 128 | bytes 2048 | tf_op jit(solution)/shard_map/neg | solution.py:435

commit v3 on v2

--- a/solution.py
+++ b/solution.py
@@ -46,12 +46,12 @@
 
 def kernel(
     cost_hbm, exit_hbm, demand_hbm, turn_hbm, weight_hbm, count_hbm, col_hbm, send_blocks_hbm,
-    out_ref,
+    z_out,
     turn_raw, exit_ref, demand_ref, cost_ref, weight_ref, count_ref, col_ref, outb_ref,
-    matrix, across, table, picked, parts, ratios, exit_dup, weighted, value_dup, demand_dup, scale, dest_w,
+    matrix, across, table, picked, parts, ratios, exit_dup, weighted, value_dup, ratio_dup, demand_dup, scale, dest_w,
     terms, scan, back_scan, keep, back_keep, local, returned, sort_v, sort_s, out_at, sum_at,
-    send, recv, z_part, z_recv,
-    load_sem, send_sem, recv_sem, z_send_sem, z_recv_sem,
+    send, recv, z_part,
+    load_sem, send_sem, recv_sem, z_send_sem, z_recv_sem, z_own_sem,
 ):
     me = lax.axis_index("dom")
     group = lax.axis_index("dest")
@@ -308,7 +308,9 @@
         for n in range(BLOCKS):
             value = value_of(chunk, n)
             value_dup[chunk, n] = value
-            ratios[n] = split(demand_dup[chunk, n] / value)
+            ratio = demand_dup[chunk, n] / value
+            ratio_dup[chunk, n] = ratio
+            ratios[n] = split(ratio)
         adjoint_message(2, chunk)
 
     def gather_back(stage, chunk):
@@ -325,9 +327,7 @@
     def _(chunk):
         gather_back(2, chunk)
         for n in range(BLOCKS):
-            value = value_dup[chunk, n]
-            load = value * back_of(chunk, n) + demand_dup[chunk, n]
-            ratios[n] = split(load / value)
+            ratios[n] = split(back_of(chunk, n) + ratio_dup[chunk, n])
         adjoint_message(3, chunk)
 
     @pl.loop(0, CHUNKS)
@@ -341,26 +341,24 @@
                 moved = value_dup[chunk, n] * back_of(chunk, n)
                 flow.append(jnp.sum(moved + demand_dup[chunk, n], axis=0, keepdims=True))
                 grad.append(jnp.sum(weight * moved, axis=0, keepdims=True))
-            z_part[g, 0:1, :] += jnp.where(low1, flow[0], flow[1])
-            z_part[g, 1:2, :] += jnp.where(low1, grad[0], grad[1])
+            z_part[g, 0:1, :] += jnp.where(low1, flow[0], flow[1]) / (DESTS * GROUPS)
+            z_part[g, 1:2, :] -= jnp.where(low1, grad[0], grad[1]) / (DESTS * GROUPS)
 
     for dz in Z_OFFSETS:
         to = (group + dz) % GROUPS
         pltpu.make_async_remote_copy(
             src_ref=z_part.at[to],
-            dst_ref=z_recv.at[group],
+            dst_ref=z_out.at[group],
             send_sem=z_send_sem,
             recv_sem=z_recv_sem,
             device_id=(me, to),
             device_id_type=MESH,
         ).start()
-    z_recv[group] = z_part[group]
-    arrived = z_recv.at[pl.ds(0, GROUPS - 1)]
+    own = pltpu.make_async_copy(z_part.at[group], z_out.at[group], z_own_sem)
+    own.start()
+    arrived = z_out.at[pl.ds(0, GROUPS - 1)]
     pltpu.make_async_copy(arrived, arrived, z_recv_sem).wait()
-    total = z_recv[0]
-    for g in range(1, GROUPS):
-        total = total + z_recv[g]
-    out_ref[...] = total / (DESTS * GROUPS)
+    own.wait()
 
     left = z_part.at[pl.ds(0, GROUPS - 1)]
     pltpu.make_async_copy(left, left, z_send_sem).wait()
@@ -374,14 +372,13 @@
 
 
 def local_part(cost, turn_weight, exit_value, demand, dest_weight, slot_count, col_ref, send_blocks):
-    vmem = pl.BlockSpec(memory_space=pltpu.VMEM)
     anywhere = pl.BlockSpec(memory_space=pl.ANY)
     f32, bf16 = jnp.float32, jnp.bfloat16
-    both = pl.pallas_call(
+    parts = pl.pallas_call(
         kernel,
-        out_shape=jax.ShapeDtypeStruct((8, PAIR), f32),
+        out_shape=jax.ShapeDtypeStruct((GROUPS, 2, PAIR), f32),
         in_specs=[anywhere] * 8,
-        out_specs=vmem,
+        out_specs=anywhere,
         scratch_shapes=[
             pltpu.VMEM((BLOCKS, BLK, SLOTS * BLK), f32),
             pltpu.VMEM((DESTS, BLOCKS * BLK), f32),
@@ -401,6 +398,7 @@
             pltpu.VMEM((BLOCKS, ROWS, PAIR), f32),
             pltpu.VMEM((CHUNKS, BLOCKS, ROWS, PAIR), f32),
             pltpu.VMEM((CHUNKS, BLOCKS, ROWS, PAIR), f32),
+            pltpu.VMEM((CHUNKS, BLOCKS, ROWS, PAIR), f32),
             pltpu.VMEM((BLOCKS, PAIR), f32),
             pltpu.VMEM((DESTS, PAIR), f32),
             pltpu.VMEM((LIVE // 2, ROWS, PAIR), f32),
@@ -416,11 +414,11 @@
             pltpu.SMEM((4 * PARTS,), jnp.int32),
             pltpu.VMEM((STAGES, CHUNKS, PARTS, ROWS, PAIR), f32),
             pltpu.VMEM((STAGES, CHUNKS, PARTS, ROWS, PAIR), f32),
-            pltpu.VMEM((GROUPS, 8, PAIR), f32),
-            pltpu.VMEM((GROUPS, 8, PAIR), f32),
+            pltpu.VMEM((GROUPS, 2, PAIR), f32),
             pltpu.SemaphoreType.DMA((8,)),
             pltpu.SemaphoreType.DMA((STAGES, CHUNKS)),
             pltpu.SemaphoreType.DMA((STAGES, CHUNKS)),
+            pltpu.SemaphoreType.DMA,
             pltpu.SemaphoreType.DMA,
             pltpu.SemaphoreType.DMA,
         ],
@@ -432,7 +430,7 @@
         cost, exit_value, demand, turn_weight, dest_weight, slot_count, col_ref.T,
         send_blocks.transpose(0, 2, 1),
     )
-    return both[0], -both[1]
+    return jnp.sum(parts[:, 0], axis=0), jnp.sum(parts[:, 1], axis=0)
 
 
 def solution(mesh):

time: 56.7 us -> 56.2 us (level)
    reduce_sum x0 -> x1, other arithmetic: none -> 1.31 us  [local_part(): return (jnp.sum(parts[:, 0], axis=0), jnp.sum(parts[:, 1], axis=0))]
    neg x1 -> x0, other arithmetic: 1.26 us -> none  [local_part(): return (both[0], -both[1])]
where the time goes in v3:
time: 56.2 us; the launch traced here: 56 us
  Pallas kernels  54.1 us (96%)
  other arithmetic  1.31 us (2%)
  between operations  0.64 us (1%)
    pallas_call x1, Pallas kernels, local_part(): pl.pallas_call(kernel, out_shape=jax.ShapeDtypeStruct((GROUPS, 2, PAIR),...  54.1 us
    reduce_sum x1, other arithmetic, local_part(): return (jnp.sum(parts[:, 0], axis=0), jnp.sum(parts[:, 1], axis=0))  1.31 us

profile of v3, /device:TPU:1, one launch (start us, length us, event | category | flops | bytes accessed | tf_op | source)
XLA Modules:
  0.0 56.0 jit_solution(4277502039202722219)
XLA Ops:
  0.6 54.1 %route_choice.1 = f32[8,2,128]{2,1,0:T(2,128)} custom-call(f32[1024]{0:T(1024)} %cost_hbm.1, f32[48,1024]{1,0:T(8,128)} %exit_hbm.1, f32[48,1024]{1,0:T(8,128)} %demand_hbm.1, f32[16,64,512]{2,1,0:T(8,128)} %turn_hbm.1, f32[48]{0:T(128)} %weight_hbm.1, s32[16]{0:T(128)} %count_hbm.1, s32[8,16]{1,0:T(8,128)} %bitcast.3, s32[32,2,32]{2,1,0:T(2,128)} %bitcast.2), custom_call_target="tpu_custom_call" | custom-call | tf_op jit(solution)/shard_map/route_choice/pallas_call | solution.py:377
  54.7 1.3 %slice_reduce_fusion = (f32[128]{0:T(128)}, f32[128]{0:T(128)}) fusion(f32[8,2,128]{2,1,0:T(2,128)} %route_choice.1), kind=kLoop, calls=%fused_computation | loop fusion | flops 1792 | bytes 9216 | tf_op jit(solution)/shard_map/reduce_sum | solution.py:433

commit v4 on v3

--- a/solution.py
+++ b/solution.py
@@ -23,13 +23,13 @@
 
 
 def hops(offset):
-    dx, dy, dc = offset
-    return min(dx, 4 - dx) + min(dy, 4 - dy) + 0.5 * dc
+    dx, dy, _ = offset
+    return min(dx, 4 - dx) + min(dy, 4 - dy)
 
 
 OFFSETS = sorted(
     ((dx, dy, dc) for dx in range(4) for dy in range(4) for dc in range(2) if dx or dy or dc),
-    key=lambda o: -hops(o),
+    key=lambda o: (-hops(o), o[2]),
 )
 Z_OFFSETS = (4, 3, 5, 2, 6, 1, 7)
 
@@ -254,7 +254,7 @@
         return jnp.where(low_half, source[sort_s[at, first]], source[sort_s[at + 1, second]])
 
     def take_received(stage, chunk):
-        @pl.loop(0, PARTS, unroll=8)
+        @pl.loop(0, PARTS, unroll=PARTS)
         def _(p):
             pair = recv[stage, chunk, p]
             table[chunk, BLOCKS + 2 * p] = split(pair)

time: 56.2 us -> 55.2 us (0.982)
  Pallas kernels: 54.1 us -> 53 us
    pallas_call x1, Pallas kernels: 54.1 us -> 53 us  [local_part(): pl.pallas_call(kernel, out_shape=jax.ShapeDtypeStruct((GROUPS, 2, PAIR),...]
where the time goes in v4:
time: 55.2 us; the launch traced here: 55 us
  Pallas kernels  53 us (96%)
  other arithmetic  1.31 us (2%)
  between operations  0.64 us (1%)
    pallas_call x1, Pallas kernels, local_part(): pl.pallas_call(kernel, out_shape=jax.ShapeDtypeStruct((GROUPS, 2, PAIR),...  53 us
    reduce_sum x1, other arithmetic, local_part(): return (jnp.sum(parts[:, 0], axis=0), jnp.sum(parts[:, 1], axis=0))  1.31 us

profile of v4, /device:TPU:1, one launch (start us, length us, event | category | flops | bytes accessed | tf_op | source)
XLA Modules:
  0.0 55.0 jit_solution(13863448530901552938)
XLA Ops:
  0.6 53.0 %route_choice.1 = f32[8,2,128]{2,1,0:T(2,128)} custom-call(f32[1024]{0:T(1024)} %cost_hbm.1, f32[48,1024]{1,0:T(8,128)} %exit_hbm.1, f32[48,1024]{1,0:T(8,128)} %demand_hbm.1, f32[16,64,512]{2,1,0:T(8,128)} %turn_hbm.1, f32[48]{0:T(128)} %weight_hbm.1, s32[16]{0:T(128)} %count_hbm.1, s32[8,16]{1,0:T(8,128)} %bitcast.3, s32[32,2,32]{2,1,0:T(2,128)} %bitcast.2), custom_call_target="tpu_custom_call" | custom-call | tf_op jit(solution)/shard_map/route_choice/pallas_call | solution.py:377
  53.7 1.3 %slice_reduce_fusion = (f32[128]{0:T(128)}, f32[128]{0:T(128)}) fusion(f32[8,2,128]{2,1,0:T(2,128)} %route_choice.1), kind=kLoop, calls=%fused_computation | loop fusion | flops 1792 | bytes 9216 | tf_op jit(solution)/shard_map/reduce_sum | solution.py:433
